TPU v7x, 32 devices: a whole 2x2x4 slice. The times are simulated.
32 devices in a mesh: groups: 2 (over y), tile: 4 (over z), mode: 2 (over x), rep: 2 (over core).
Axes of the slice: x: 2, y: 2, z: 4, core: 2. Of those that a mesh axis runs over, the one named last changes fastest.
Arguments:
- object_tiles: bfloat16 [2, 4096, 640], P(None, ('groups', 'tile', 'mode', 'rep')), parts along dimension 1, may hold values from -3 to 3
- probe_modes: bfloat16 [4, 2, 512, 512], P(('groups', 'mode')), parts along dimension 0, may hold values from -3 to 3
- measured: float32 [16, 512, 512], P(('groups', 'tile', 'rep')), parts along dimension 0, may hold values from 0.5 to 3
- row_offset: int32 [16], P(('groups', 'tile', 'rep')), parts along dimension 0, may hold values from 0 to 511
- col_offset: int32 [16], P(('groups', 'tile', 'rep')), parts along dimension 0, may hold values from 0 to 128
Outputs:
- object_grad: float32 [2, 4096, 640], P(None, ('groups', 'tile', 'mode', 'rep')), parts along dimension 1
- probe_grad: float32 [4, 2, 512, 512], P(('groups', 'mode')), parts along dimension 0
There are 2 independent parts, one for each index of `groups`. A program takes and returns all parts, laid end to end along the dimension named above; each array names one. Nothing has to cross between parts.
All inputs are finite; a program needn't handle non-finite values.
Results may differ from a plain program's by a relative error of at most 0.013.
Values may be sent and summed in bfloat16 or wider, within the bound.
A program may use at most 64 MiB of HBM per device.

v0:
```python
import math

import jax
import jax.numpy as jnp
from jax import lax
from jax.sharding import PartitionSpec as P

PATCH = 512


def passed_along(value, axis, steps):
    count = lax.axis_size(axis)
    initial, last = (max(0, -steps), min(count, count - steps))
    return lax.ppermute(value, axis, [(source, source + steps) for source in range(initial, last)])


def dft_tables(points):
    indices = jnp.arange(points, dtype=jnp.int32)
    products = indices[:, None] * indices[None, :] % points
    angles = products.astype(jnp.float32) * (2.0 * math.pi / points)
    norm_factor = 1.0 / math.sqrt(points)
    cos_table = (jnp.cos(angles) * norm_factor).astype(jnp.bfloat16)
    sin_table = (jnp.sin(angles) * norm_factor).astype(jnp.bfloat16)
    forward_left = jnp.concatenate(
        [jnp.concatenate([cos_table, sin_table], 1), jnp.concatenate([-sin_table, cos_table], 1)], 0
    )
    inverse_left = jnp.concatenate(
        [jnp.concatenate([cos_table, -sin_table], 1), jnp.concatenate([sin_table, cos_table], 1)], 0
    )
    return (cos_table, sin_table, forward_left, inverse_left)


def column_pass(left_matrix, stacked):
    points = stacked.shape[-1]
    product = jnp.dot(
        left_matrix, stacked.reshape(2 * points, points), preferred_element_type=jnp.float32
    )
    return product.reshape(2, points, points)


def row_pass(stacked, cos_table, sin_table, sign_flip):
    points = stacked.shape[-1]
    flattened = stacked.reshape(2 * points, points)
    with_cos = jnp.dot(flattened, cos_table, preferred_element_type=jnp.float32).reshape(
        2, points, points
    )
    with_sin = jnp.dot(flattened, sin_table, preferred_element_type=jnp.float32).reshape(
        2, points, points
    )
    real_part = with_cos[0] + sign_flip * with_sin[1]
    imag_part = with_cos[1] - sign_flip * with_sin[0]
    return jnp.stack([real_part, imag_part])


def forward_wave(exit_wave, tables):
    cos_table, sin_table, forward_left, inverse_left = tables
    middle = column_pass(forward_left, exit_wave).astype(jnp.bfloat16)
    return row_pass(middle, cos_table, sin_table, 1.0)


def inverse_wave(corrected, tables):
    cos_table, sin_table, forward_left, inverse_left = tables
    middle = column_pass(inverse_left, corrected).astype(jnp.bfloat16)
    return row_pass(middle, cos_table, sin_table, -1.0)


def complex_times(first, second):
    real_part = first[0] * second[0] - first[1] * second[1]
    imag_part = first[0] * second[1] + first[1] * second[0]
    return jnp.stack([real_part, imag_part])


def conj_times(first, second):
    real_part = first[0] * second[0] + first[1] * second[1]
    imag_part = first[0] * second[1] - first[1] * second[0]
    return jnp.stack([real_part, imag_part])


def local(object_tiles, probe_modes, measured, row_offset, col_offset):
    tables = dft_tables(PATCH)
    own_rows = lax.all_gather(object_tiles, ("mode", "rep"), axis=1, tiled=True)
    next_rows = passed_along(own_rows, "tile", -1)
    extended = jnp.concatenate([own_rows, next_rows], axis=1)
    tile_rows = own_rows.shape[1]
    obj_cols = extended.shape[2]
    zero_index = jnp.zeros((), jnp.int32)
    row_start = row_offset[0]
    col_start = col_offset[0]
    obj_patch = lax.dynamic_slice(
        extended, (zero_index, row_start, col_start), (2, PATCH, PATCH)
    ).astype(jnp.float32)
    probe_float = probe_modes[0].astype(jnp.float32)
    exit_wave = complex_times(probe_float, obj_patch).astype(jnp.bfloat16)
    spectra = forward_wave(exit_wave, tables)
    local_power = spectra[0] ** 2 + spectra[1] ** 2
    intensity = lax.psum(local_power.astype(jnp.bfloat16), "mode").astype(jnp.float32)
    factor = 1.0 - measured[0] / jnp.sqrt(jnp.maximum(intensity, 1.0))
    corrected = (spectra * factor).astype(jnp.bfloat16)
    back_wave = inverse_wave(corrected, tables)
    obj_term = conj_times(probe_float, back_wave).astype(jnp.bfloat16).astype(jnp.float32)
    extended_term = jnp.zeros((2, 2 * tile_rows, obj_cols), jnp.float32)
    extended_term = lax.dynamic_update_slice(
        extended_term, obj_term, (zero_index, row_start, col_start)
    )
    own_sum, next_sum = (
        lax.psum_scatter(
            extended_term[:, :tile_rows].astype(jnp.bfloat16),
            ("mode", "rep"),
            scatter_dimension=1,
            tiled=True,
        ).astype(jnp.float32),
        lax.psum_scatter(
            extended_term[:, tile_rows:].astype(jnp.bfloat16),
            ("mode", "rep"),
            scatter_dimension=1,
            tiled=True,
        ).astype(jnp.float32),
    )
    carried = passed_along(next_sum.astype(jnp.bfloat16), "tile", 1).astype(next_sum.dtype)
    object_grad = own_sum + carried
    probe_term = conj_times(obj_patch, back_wave)
    probe_grad = lax.psum(probe_term.astype(jnp.bfloat16), ("tile", "rep")).astype(jnp.float32)
    return (object_grad, probe_grad[None])


def solution(mesh):
    placed = (
        P(None, ("groups", "tile", "mode", "rep"), None),
        P(("groups", "mode"), None, None, None),
        P(("groups", "tile", "rep"), None, None),
        P(("groups", "tile", "rep")),
        P(("groups", "tile", "rep")),
    )
    return jax.shard_map(
        local,
        mesh=mesh,
        in_specs=placed,
        out_specs=(
            P(None, ("groups", "tile", "mode", "rep"), None),
            P(("groups", "mode"), None, None, None),
        ),
        check_vma=False,
    )
```

profile of v0, /device:TPU:0, one launch (start us, length us, event | category | flops | bytes accessed | tf_op | source)
XLA Modules:
  0.0 272.0 jit_solution(3670676956302794017)
XLA Ops:
  7.2 0.0 all-gather.2.cloned.1.call-start
  7.2 0.7 all-gather.2.cloned.1.call-update
  7.9 0.0 all-reduce.3.cloned.1.call-start
  7.9 22.5 %all-gather.2.cloned.1.call-done = bf16[2,512,640]{2,1,0:T(8,128)(2,1)} async-done(((bf16[2,128,640]{2,1,0:T(8,128)(2,1)}), bf16[2,512,640]{2,1,0:T(8,128)(2,1)}) %all-gather.2.cloned.1.call-update) | async-done | bytes 1310736 | tf_op jit(solution)/shard_map/all_gather | solution.py:81
  30.5 1.3 collective-permute-start
  33.1 2.9 %convert_element_type.110 = f32[1,2,512,512]{3,2,1,0:T(8,128)} convert(bf16[1,2,512,512]{3,2,1,0:T(8,128)(2,1)} %param.6) | non-fusion elementwise | flops 524288 | bytes 3145728 | tf_op jit(solution)/shard_map/convert_element_type | solution.py:92
  35.9 4.0 %fusion.18 = bf16[512,512]{1,0:T(8,128)(2,1)S(1)} fusion(), kind=kLoop, calls=%fused_computation.50 | loop fusion | flops 4980736 | bytes 524288 | tf_op jit(solution)/shard_map/neg | solution.py:28
  39.9 4.4 %multiply_convert_fusion = (bf16[512,512]{1,0:T(8,128)(2,1)S(1)}, bf16[512,512]{1,0:T(8,128)(2,1)S(1)}) fusion(), kind=kLoop, calls=%fused_computation.42 | loop fusion | flops 4718592 | bytes 1048576 | tf_op jit(solution)/shard_map/convert_element_type | solution.py:23
  44.3 0.0 copy-start.4
  44.3 9.7 %fusion.1 = (bf16[1024,1024]{1,0:T(8,128)(2,1)S(1)}, bf16[1024,1024]{1,0:T(8,128)(2,1)}) fusion(bf16[512,512]{1,0:T(8,128)(2,1)S(1)} %get-tuple-element.18, bf16[512,512]{1,0:T(8,128)(2,1)S(1)} %fusion.18, bf16[512,512]{1,0:T(8,128)(2,1)S(1)} %get-tuple-element.17), kind=kLoop, calls=%fused_computation.7 | loop fusion | flops 14680064 | bytes 5767168 | tf_op jit(solution)/shard_map/concatenate | solution.py:24
  54.1 9.4 %collective-permute-done = bf16[2,512,640]{2,1,0:T(8,128)(2,1)S(1)} collective-permute-done((bf16[2,512,640]{2,1,0:T(8,128)(2,1)}, bf16[2,512,640]{2,1,0:T(8,128)(2,1)S(1)}, u32[]{:S(2)}, u32[]{:S(2)}) %collective-permute-start) | collective-permute-done | bytes 1310752 | tf_op jit(solution)/shard_map/ppermute | solution.py:14
  63.5 1.7 fusion.7
  65.2 0.6 subtract_convert_fusion.2
  65.8 0.1 pad_maximum_fusion.4
  65.9 1.2 convolution_convert_fusion.1
  67.2 5.7 %fusion.17 = f32[1024,512]{1,0:T(8,128)S(1)} fusion(bf16[1024,512]{1,0:T(8,128)(2,1)S(1)} %bitcast.66), kind=kOutput, calls=%fused_computation.49 | convolution fusion | flops 541065216 | bytes 3145728 | tf_op jit(solution)/shard_map/dot_general | solution.py:47
  72.8 5.8 %fusion.20 = f32[1024,512]{1,0:T(8,128)S(1)} fusion(bf16[1024,512]{1,0:T(8,128)(2,1)S(1)} %bitcast.67), kind=kOutput, calls=%fused_computation.52 | convolution fusion | flops 541065216 | bytes 3145728 | tf_op jit(solution)/shard_map/dot_general | solution.py:44
  78.7 1.7 add_convert_fusion.2
  80.3 0.0 all-reduce.3.cloned.1.call-update
  80.4 0.0 reduce-scatter.5.cloned.1.call-start
  80.4 27.8 %all-reduce.3.cloned.1.call-done = bf16[512,512]{1,0:T(8,128)(2,1)} async-done(((bf16[512,512]{1,0:T(8,128)(2,1)}), bf16[512,512]{1,0:T(8,128)(2,1)}) %all-reduce.3.cloned.1.call-update) | async-done | bytes 524304 | tf_op jit(solution)/shard_map/psum | solution.py:96
  108.2 1.6 fusion.12
  109.8 0.1 copy-done.2
  109.9 0.4 fusion.2
  110.3 1.1 copy-done.3
  111.5 1.3 convolution_convert_fusion
  112.7 5.7 %fusion.16 = f32[1024,512]{1,0:T(8,128)S(1)} fusion(bf16[1024,512]{1,0:T(8,128)(2,1)S(1)} %bitcast.68), kind=kOutput, calls=%fused_computation.48 | convolution fusion | flops 541065216 | bytes 3145728 | tf_op jit(solution)/shard_map/dot_general | solution.py:47
  118.4 5.6 %fusion.19 = f32[1024,512]{1,0:T(8,128)S(1)} fusion(bf16[1024,512]{1,0:T(8,128)(2,1)S(1)} %bitcast.69), kind=kOutput, calls=%fused_computation.51 | convolution fusion | flops 541065216 | bytes 3145728 | tf_op jit(solution)/shard_map/dot_general | solution.py:44
  124.1 0.8 add_convert_fusion
  124.9 0.8 copy-done.1
  125.7 1.7 add_convert_fusion.1
  127.3 1.1 maximum_convert_fusion
  128.4 0.2 broadcast_in_dim.12
  128.6 17.0 %dynamic_update_slice.3 = bf16[2,1024,640]{2,1,0:T(8,128)(2,1)S(1)} dynamic-update-slice(bf16[2,1024,640]{2,1,0:T(8,128)(2,1)S(1)} %broadcast_in_dim.12, bf16[2,512,512]{2,1,0:T(8,128)(2,1)} %maximum_convert_fusion, s32[]{:T(128)} %constant.11.clone.1, s32[]{:T(128)S(6)} %select_n.38, s32[]{:T(128)S(6)} %select_n.39) | dynamic-update-slice | bytes 2097156 | tf_op jit(solution)/shard_map/dynamic_update_slice | solution.py:102
  145.5 1.7 fusion.45
  147.3 0.0 reduce-scatter.5.cloned.1.call-update
  147.3 0.0 all-reduce.5.cloned.1.call-start
  147.3 2.1 maximum_bitcast_fusion
  149.5 0.0 all-reduce.5.cloned.1.call-update
  149.5 0.0 reduce-scatter.3.cloned.1.call-start
  149.5 0.5 reduce-scatter.3.cloned.1.call-update
  150.1 23.9 %reduce-scatter.5.cloned.1.call-done = bf16[2,128,640]{2,1,0:T(8,128)(2,1)} async-done(((bf16[2,512,640]{2,1,0:T(8,128)(2,1)}), bf16[2,128,640]{2,1,0:T(8,128)(2,1)}) %reduce-scatter.5.cloned.1.call-update) | async-done | bytes 327696 | tf_op jit(solution)/shard_map/reduce_scatter | solution.py:112
  174.0 3.4 %collective-permute-start.1 = (bf16[2,128,640]{2,1,0:T(8,128)(2,1)}, bf16[2,128,640]{2,1,0:T(8,128)(2,1)S(1)}, u32[]{:S(2)}, u32[]{:S(2)}) collective-permute-start(bf16[2,128,640]{2,1,0:T(8,128)(2,1)} %reduce-scatter.5.cloned.1.call-done), channel_id=1, source_target_pairs={{0,4},{4,8},{8,12},{1,5},{5,9},{9,13},{2,6},{6,10},{10,14},{3,7},{... | collective-permute-start | bytes 983048 | tf_op jit(solution)/shard_map/ppermute | solution.py:14
  177.4 58.3 %all-reduce.5.cloned.1.call-done = bf16[1,2,512,512]{3,2,1,0:T(8,128)(2,1)} async-done(((bf16[1,2,512,512]{3,2,1,0:T(8,128)(2,1)}), bf16[1,2,512,512]{3,2,1,0:T(8,128)(2,1)}) %all-reduce.5.cloned.1.call-update) | async-done | bytes 1048592 | tf_op jit(solution)/shard_map/psum | solution.py:122
  235.7 2.8 %broadcast_in_dim.14 = f32[1,2,512,512]{3,2,1,0:T(8,128)} convert(bf16[1,2,512,512]{3,2,1,0:T(8,128)(2,1)} %all-reduce.5.cloned.1.call-done) | non-fusion elementwise | flops 524288 | bytes 3145728 | tf_op jit(solution)/shard_map/broadcast_in_dim | solution.py:123
  238.5 25.1 %reduce-scatter.3.cloned.1.call-done = bf16[2,128,640]{2,1,0:T(8,128)(2,1)} async-done(((bf16[2,512,640]{2,1,0:T(8,128)(2,1)}), bf16[2,128,640]{2,1,0:T(8,128)(2,1)}) %reduce-scatter.3.cloned.1.call-update) | async-done | bytes 327696 | tf_op jit(solution)/shard_map/reduce_scatter | solution.py:106
  263.6 0.0 collective-permute-done.1
  263.6 1.9 convert_add_fusion
  (6 shorter events, 0.0 us)
Async XLA Ops:
  7.2 23.3 %all-gather.2.cloned.1.call-start = ((), (), s32[]{:S(2)}) async-start(), calls=%async_computation.2 | async-start | bytes 1638400 | tf_op jit(solution)/shard_map/all_gather | solution.py:81
  7.9 100.3 %all-reduce.3.cloned.1.call-start = ((), (), s32[]{:S(2)}) async-start(), calls=%async_computation.3 | async-start | bytes 1048576 | tf_op jit(solution)/shard_map/psum | solution.py:96
  30.5 33.0 %collective-permute-start = (bf16[2,512,640]{2,1,0:T(8,128)(2,1)}, bf16[2,512,640]{2,1,0:T(8,128)(2,1)S(1)}, u32[]{:S(2)}, u32[]{:S(2)}) collective-permute-start(bf16[2,512,640]{2,1,0:T(8,128)(2,1)} %all-gather.2.cloned.1.call-done), channel_id=1, source_target_pairs={{4,0},{8,4},{12,8},{5,1},{9,5},{13,9},{6,2},{10,6},{14,10},{7,3},{... | collective-permute-start | bytes 3932168 | tf_op jit(solution)/shard_map/ppermute | solution.py:14
  44.3 19.2 %copy-start.4 = (bf16[2,512,640]{2,1,0:T(8,128)(2,1)S(1)}, bf16[2,512,640]{2,1,0:T(8,128)(2,1)}, u32[]{:S(2)}) copy-start(bf16[2,512,640]{2,1,0:T(8,128)(2,1)} %all-gather.2.cloned.1.call-done) | copy-start | bytes 3932164
  54.1 11.2 %copy-start = (f32[1,2,512,512]{3,2,1,0:T(8,128)S(1)}, f32[1,2,512,512]{3,2,1,0:T(8,128)}, u32[]{:S(2)}) copy-start(f32[1,2,512,512]{3,2,1,0:T(8,128)} %convert_element_type.110) | copy-start | bytes 6291460
  80.4 93.6 %reduce-scatter.5.cloned.1.call-start = ((), (), s32[]{:S(2)}) async-start(), calls=%async_computation.5 | async-start | bytes 1638400 | tf_op jit(solution)/shard_map/reduce_scatter | solution.py:112
  108.2 1.7 copy-start.2
  109.9 1.6 copy-start.3
  124.1 1.6 copy-start.1
  147.3 88.4 %all-reduce.5.cloned.1.call-start = ((), (), s32[]{:S(2)}) async-start(), calls=%async_computation.6 | async-start | bytes 2097152 | tf_op jit(solution)/shard_map/psum | solution.py:122
  149.5 114.1 %reduce-scatter.3.cloned.1.call-start = ((), (), s32[]{:S(2)}) async-start(), calls=%async_computation.4 | async-start | bytes 1638400 | tf_op jit(solution)/shard_map/reduce_scatter | solution.py:106
  174.0 89.6 %collective-permute-start.1 = (bf16[2,128,640]{2,1,0:T(8,128)(2,1)}, bf16[2,128,640]{2,1,0:T(8,128)(2,1)S(1)}, u32[]{:S(2)}, u32[]{:S(2)}) collective-permute-start(bf16[2,128,640]{2,1,0:T(8,128)(2,1)} %reduce-scatter.5.cloned.1.call-done), channel_id=1, source_target_pairs={{0,4},{4,8},{8,12},{1,5},{5,9},{9,13},{2,6},{6,10},{10,14},{3,7},{... | collective-permute-start | bytes 983048 | tf_op jit(solution)/shard_map/ppermute | solution.py:14
Sparse Core Ops, SparseCore 0:
  9.6 20.8 all-gather.1
  80.5 27.6 all-reduce.2
  147.4 26.5 reduce-scatter.4
  176.2 59.4 all-reduce.4
  238.1 25.4 reduce-scatter.2
where the time goes:
time: 273 us; the launch traced here: 272 us
  waiting for transfers between devices  168 us (62%)
  other arithmetic  37.5 us (14%)
  matrix products  25.3 us (9%)
  local copies, waits for them, and re-layouts  20.8 us (8%)
  between operations  15.2 us (6%)
  starting transfers between devices  4.86 us (2%)
    psum x1, waiting for transfers between devices, local(): lax.psum(probe_term.astype(jnp.bfloat16), ('tile', 'rep'))  58.3 us
    psum x1, waiting for transfers between devices, local(): lax.psum(local_power.astype(jnp.bfloat16), 'mode').astype(jnp.float32)  27.8 us
    reduce_scatter x1, waiting for transfers between devices, local(): lax.psum_scatter(extended_term[:, :tile_rows].astype(jnp.bfloat16), ('mod...  25.1 us
    reduce_scatter x1, waiting for transfers between devices, local(): lax.psum_scatter(extended_term[:, tile_rows:].astype(jnp.bfloat16), ('mod...  23.9 us
    all_gather x1, waiting for transfers between devices, local(): own_rows = lax.all_gather(object_tiles, ('mode', 'rep'), axis=1, tiled=True)  22.5 us
    dynamic_update_slice x1, local copies, waits for them, and re-layouts, local(): lax.dynamic_update_slice(extended_term, obj_term, (zero_index, row_start,...  17 us
    dot_general x2, matrix products, row_pass(): jnp.dot(flattened, cos_table, preferred_element_type=jnp.float32)  11.5 us
    dot_general x2, matrix products, row_pass(): jnp.dot(flattened, sin_table, preferred_element_type=jnp.float32)  11.3 us
  transfers between devices with their start and end apart: 7, of which 6 were waited for; matrix products, arithmetic and copies ran while one was open for 10% of the time, Pallas kernels for 0%

commit v1 on v0

--- a/solution.py
+++ b/solution.py
@@ -1,12 +1,18 @@
+import functools
 import math
 
 import jax
 import jax.numpy as jnp
+import numpy as np
 from jax import lax
+from jax.experimental import pallas as pl
+from jax.experimental.pallas import tpu as pltpu
 from jax.sharding import PartitionSpec as P
 
 PATCH = 512
-
+F32, BF16 = jnp.float32, jnp.bfloat16
+POWER_ROWS = 128
+CHAIN_PARTS = 4
 
 def passed_along(value, axis, steps):
     count = lax.axis_size(axis)
@@ -123,6 +129,514 @@
     return (object_grad, probe_grad[None])
 
 
+def cos_sin_tables(points):
+    products = np.outer(np.arange(points), np.arange(points)) % points
+    angles = products * (2.0 * math.pi / points)
+    norm_factor = 1.0 / math.sqrt(points)
+    return (
+        (np.cos(angles) * norm_factor).astype(jnp.bfloat16),
+        (np.sin(angles) * norm_factor).astype(jnp.bfloat16),
+    )
+
+
+def matmul(left, right):
+    return jnp.dot(left, right, preferred_element_type=F32)
+
+
+def rows_at(start, size):
+    return pl.ds(pl.multiple_of(start, size), size)
+
+
+def fused_kernel(
+    tiles, row_ref, col_ref, obj, probe, cos_ref, sin_ref, measured, object_out, probe_out,
+    ext, shift_out, shift_in, rotate, rotate_back, left_fwd, right_fwd, right_inv, left_inv,
+    probe_rot, patch, wave, middle, spec, power, power_in, back_stack, term, term_in,
+    probe_term, half_out, half_in, half_sum, up_left, up_right, up_out, down, down_in,
+    placed_out, placed_mine, placed_in, carry_out, carry_in,
+    g_send, g_recv, s_send, s_recv, pw_send, pw_recv, t_send, t_recv, h_send, h_recv,
+    up_send, up_recv, dn_send, dn_recv, sib_send, sib_recv, pl_send, pl_recv, c_send, c_recv,
+):
+    t, m, r = lax.axis_index("tile"), lax.axis_index("mode"), lax.axis_index("rep")
+    sibling, partner = {"rep": 1 - r}, {"mode": 1 - m}
+    lower, upper = {"tile": t - 1}, {"tile": t + 1}
+    has_lower, has_upper = t > 0, t < tiles - 1
+    height, width = obj.shape[1], obj.shape[2]
+    points = probe.shape[-1]
+    row_start, col_start = row_ref[0], col_ref[0]
+
+    def copy(src, dst, send, recv, device):
+        return pltpu.make_async_remote_copy(
+            src_ref=src, dst_ref=dst, send_sem=send, recv_sem=recv,
+            device_id=device, device_id_type=pl.DeviceIdType.MESH,
+        )
+
+    barrier = pltpu.get_barrier_semaphore()
+    for device in (sibling, partner):
+        pl.semaphore_signal(barrier, inc=1, device_id=device, device_id_type=pl.DeviceIdType.MESH)
+
+    @pl.when(has_lower)
+    def _():
+        pl.semaphore_signal(barrier, inc=1, device_id=lower, device_id_type=pl.DeviceIdType.MESH)
+
+    @pl.when(has_upper)
+    def _():
+        pl.semaphore_signal(barrier, inc=1, device_id=upper, device_id_type=pl.DeviceIdType.MESH)
+
+    peers = 2 + has_lower.astype(jnp.int32) + has_upper.astype(jnp.int32)
+    pl.semaphore_wait(barrier, peers)
+
+    own_slot, other_slot = 2 * m + r, 2 * (1 - m) + r
+
+    def gather(kind, part, src, slot, device):
+        return copy(src, ext.at[slot, part], g_send.at[kind, part], g_recv.at[kind, part], device)
+
+    def block(slot, part):
+        return ext.at[slot, part]
+
+    def to_sibling(part):
+        return gather(0, part, obj.at[part], own_slot, sibling)
+
+    def to_partner(part):
+        return gather(1, part, obj.at[part], own_slot, partner)
+
+    def to_lower(part):
+        return gather(2, part, obj.at[part], 4 + own_slot, lower)
+
+    def relay_partner(part):
+        return gather(3, part, block(other_slot, part), other_slot, sibling)
+
+    def relay_upper(part):
+        return gather(4, part, block(4 + own_slot, part), 4 + own_slot, sibling)
+
+    def cross_partner(part):
+        return gather(5, part, block(4 + own_slot, part), 4 + own_slot, partner)
+
+    def cross_lower(part):
+        return gather(5, part, block(other_slot, part), 4 + other_slot, lower)
+
+    def relay_cross(part):
+        return gather(6, part, block(4 + other_slot, part), 4 + other_slot, sibling)
+
+    for part in range(2):
+        to_partner(part).start()
+
+        @pl.when(has_lower)
+        def _():
+            to_lower(part).start()
+
+        to_sibling(part).start()
+    shift_out[...] = jnp.full(shift_out.shape, row_start, jnp.int32)
+    send_shift = copy(shift_out, shift_in, s_send, s_recv, sibling)
+    send_shift.start()
+
+    first = lax.broadcasted_iota(jnp.int32, (points, points), 0)
+    second = lax.broadcasted_iota(jnp.int32, (points, points), 1)
+    apart = first - second - row_start
+    rotate[...] = jnp.where((apart == 0) | (apart == -points), 1.0, 0.0).astype(BF16)
+    apart = second - first - row_start
+    rotate_back[...] = jnp.where((apart == 0) | (apart == -points), 1.0, 0.0).astype(BF16)
+    cosine, sine = cos_ref[...], sin_ref[...]
+    minus = -sine
+    right_fwd[:points, :points] = cosine
+    right_fwd[:points, points:] = minus
+    right_fwd[points:, :points] = sine
+    right_fwd[points:, points:] = cosine
+    right_inv[:points, :points] = cosine
+    right_inv[:points, points:] = sine
+    right_inv[points:, :points] = minus
+    right_inv[points:, points:] = cosine
+
+    @pl.loop(0, 4)
+    def _(step):
+        rows = rows_at(step * 128, 128)
+        low = rows_at(points + step * 128, 128)
+        turn = rotate[rows, :]
+        cos_rot = matmul(turn, cos_ref[...]).astype(BF16)
+        sin_rot = matmul(turn, sin_ref[...]).astype(BF16)
+        left_inv[rows, :points] = cos_rot
+        left_inv[rows, points:] = -sin_rot
+        left_inv[low, :points] = sin_rot
+        left_inv[low, points:] = cos_rot
+        cos_turn = matmul(cos_ref[rows, :], rotate_back[...]).astype(BF16)
+        sin_turn = matmul(sin_ref[rows, :], rotate_back[...]).astype(BF16)
+        left_fwd[rows, :points] = cos_turn
+        left_fwd[rows, points:] = sin_turn
+        left_fwd[low, :points] = -sin_turn
+        left_fwd[low, points:] = cos_turn
+        for part in range(2):
+            probe_rot[part, rows, :] = matmul(turn, probe[0, part]).astype(BF16)
+
+    ext[own_slot] = obj[...]
+
+    @pl.when(jnp.logical_not(has_upper))
+    def _():
+        ext[4:8] = jnp.zeros((4, 2, height, width), BF16)
+
+    @pl.when(t == 0)
+    def _():
+        up_left[...] = jnp.zeros_like(up_left)
+
+    @pl.when(t == tiles - 1)
+    def _():
+        up_right[...] = jnp.zeros_like(up_right)
+
+    for part in range(2):
+        gather(1, part, obj.at[part], other_slot, partner).wait_recv()
+        relay_partner(part).start()
+
+        @pl.when((r == 1) & has_lower)
+        def _():
+            cross_lower(part).start()
+
+        @pl.when(has_upper)
+        def _():
+            gather(2, part, obj.at[part], 4 + own_slot, lower).wait_recv()
+            relay_upper(part).start()
+
+            @pl.when(r == 0)
+            def _():
+                cross_partner(part).start()
+
+    for part in range(2):
+        @pl.when(has_upper)
+        def _():
+            gather(5, part, obj.at[part], 4 + other_slot, partner).wait_recv()
+            relay_cross(part).start()
+
+    for part in range(2):
+        to_sibling(part).wait()
+        to_partner(part).wait_send()
+        relay_partner(part).wait()
+
+        @pl.when(has_lower)
+        def _():
+            to_lower(part).wait_send()
+
+        @pl.when((r == 1) & has_lower)
+        def _():
+            cross_lower(part).wait_send()
+
+        @pl.when(has_upper)
+        def _():
+            relay_upper(part).wait()
+            relay_cross(part).wait()
+
+        @pl.when((r == 0) & has_upper)
+        def _():
+            cross_partner(part).wait_send()
+
+    pick = lax.broadcasted_iota(jnp.int32, (width, points), 0) - lax.broadcasted_iota(
+        jnp.int32, (width, points), 1
+    )
+    pick = jnp.where(pick == col_start, 1.0, 0.0).astype(BF16)
+
+    @pl.loop(0, 4)
+    def _(step):
+        rows = rows_at(step * height, height)
+        low = rows_at(points + step * height, height)
+        line = lax.broadcasted_iota(jnp.int32, (height, width), 0) + step * height
+        parts = []
+        for part in range(2):
+            chosen = jnp.where(
+                line >= row_start, ext[step, part].astype(F32), ext[4 + step, part].astype(F32)
+            )
+            parts.append(matmul(chosen.astype(BF16), pick))
+            patch[part, rows, :] = parts[part].astype(BF16)
+        obj_re, obj_im = parts
+        prb_re, prb_im = (probe_rot[part, rows, :].astype(F32) for part in range(2))
+        wave[rows, :] = (prb_re * obj_re - prb_im * obj_im).astype(BF16)
+        wave[low, :] = (prb_re * obj_im + prb_im * obj_re).astype(BF16)
+
+    @pl.loop(0, 2)
+    def _(step):
+        rows = rows_at(step * 256, 256)
+        low = rows_at(points + step * 256, 256)
+        middle[rows, :points] = matmul(left_fwd[rows, :], wave[...]).astype(BF16)
+        middle[rows, points:] = matmul(left_fwd[low, :], wave[...]).astype(BF16)
+
+    def send_power(step):
+        return copy(
+            power.at[step], power_in.at[step], pw_send.at[step], pw_recv.at[step], partner
+        )
+
+    steps = points // POWER_ROWS
+
+    @pl.loop(0, steps)
+    def _(step):
+        rows = rows_at(step * POWER_ROWS, POWER_ROWS)
+        wide = matmul(middle[rows, :], right_fwd[...])
+        spec[rows, :] = wide
+        power[step] = (wide[:, :points] ** 2 + wide[:, points:] ** 2).astype(BF16)
+        send_power(step).start()
+
+    @pl.loop(0, steps)
+    def _(step):
+        rows = rows_at(step * POWER_ROWS, POWER_ROWS)
+        low = rows_at(points + step * POWER_ROWS, POWER_ROWS)
+        send_power(step).wait()
+        spec_re, spec_im = spec[rows, :points], spec[rows, points:]
+        intensity = spec_re**2 + spec_im**2 + power_in[step].astype(F32)
+        factor = 1.0 - measured[0, rows, :] / jnp.sqrt(jnp.maximum(intensity, 1.0))
+        corrected = jnp.concatenate(
+            [(spec_re * factor).astype(BF16), (spec_im * factor).astype(BF16)], 1
+        )
+        turned = matmul(corrected, right_inv[...]).astype(BF16)
+        back_stack[rows, :] = turned[:, :points]
+        back_stack[low, :] = turned[:, points:]
+
+    def send_term(step):
+        return copy(
+            term.at[2 * (1 - m) + step], term_in.at[step], t_send.at[step], t_recv.at[step], partner
+        )
+
+    @pl.loop(0, 4)
+    def _(step):
+        slot = (step + 2 * (1 - m)) % 4
+        rows = rows_at(slot * height, height)
+        low = rows_at(points + slot * height, height)
+        back_re = matmul(left_inv[rows, :], back_stack[...])
+        back_im = matmul(left_inv[low, :], back_stack[...])
+        prb_re, prb_im = (probe_rot[part, rows, :].astype(F32) for part in range(2))
+        term[slot, 0] = (prb_re * back_re + prb_im * back_im).astype(BF16)
+        term[slot, 1] = (prb_re * back_im - prb_im * back_re).astype(BF16)
+
+        @pl.when(step < 2)
+        def _():
+            send_term(step).start()
+
+        obj_re, obj_im = (patch[part, rows, :].astype(F32) for part in range(2))
+        probe_term[rows, :points] = (obj_re * back_re + obj_im * back_im).astype(BF16)
+        probe_term[rows, points:] = (obj_re * back_im - obj_im * back_re).astype(BF16)
+
+    half = points // 2
+    chunk = half // CHAIN_PARTS
+    half_out[...] = matmul(rotate_back[rows_at((1 - r) * half, half), :], probe_term[...]).astype(BF16)
+    send_half = copy(half_out, half_in, h_send, h_recv, sibling)
+    send_half.start()
+    half_sum[...] = matmul(rotate_back[rows_at(r * half, half), :], probe_term[...])
+    send_half.wait()
+    half_sum[...] += half_in[...].astype(F32)
+    root = tiles // 2
+
+    def part_rows(index):
+        return pl.ds(index * chunk, chunk)
+
+    def up_to_upper(index):
+        rows = part_rows(index)
+        return copy(up_out.at[rows], up_left.at[rows], up_send.at[index], up_recv.at[0, index], upper)
+
+    def up_to_lower(index):
+        rows = part_rows(index)
+        return copy(up_out.at[rows], up_right.at[rows], up_send.at[index], up_recv.at[1, index], lower)
+
+    def down_to_upper(index):
+        rows = part_rows(index)
+        return copy(down.at[rows], down.at[rows], dn_send.at[0, index], dn_recv.at[index], upper)
+
+    def down_to_lower(index):
+        rows = part_rows(index)
+        return copy(down.at[rows], down.at[rows], dn_send.at[1, index], dn_recv.at[index], lower)
+
+    def down_to_sibling(index):
+        rows = part_rows(index)
+        return copy(down.at[rows], down_in.at[rows], sib_send.at[index], sib_recv.at[index], sibling)
+
+    for index in range(CHAIN_PARTS):
+        rows = part_rows(index)
+
+        @pl.when((t <= root) & has_lower)
+        def _():
+            up_to_upper(index).wait_recv()
+
+        @pl.when((t >= root) & has_upper)
+        def _():
+            up_to_lower(index).wait_recv()
+
+        @pl.when(t < root)
+        def _():
+            up_out[rows] = (half_sum[rows] + up_left[rows].astype(F32)).astype(BF16)
+            up_to_upper(index).start()
+
+        @pl.when(t > root)
+        def _():
+            up_out[rows] = (half_sum[rows] + up_right[rows].astype(F32)).astype(BF16)
+            up_to_lower(index).start()
+
+        @pl.when(t == root)
+        def _():
+            down[rows] = (
+                half_sum[rows] + up_left[rows].astype(F32) + up_right[rows].astype(F32)
+            ).astype(BF16)
+
+            @pl.when(has_lower)
+            def _():
+                down_to_lower(index).start()
+
+            @pl.when(has_upper)
+            def _():
+                down_to_upper(index).start()
+
+            down_to_sibling(index).start()
+
+    place = lax.broadcasted_iota(jnp.int32, (points, width), 1) - lax.broadcasted_iota(
+        jnp.int32, (points, width), 0
+    )
+    place = jnp.where(place == col_start, 1.0, 0.0).astype(BF16)
+    send_placed = copy(placed_out, placed_in, pl_send, pl_recv, sibling)
+    for step in range(2):
+        send_term(step).wait()
+    for step in range(2):
+        which = 1 - r if step == 0 else r
+        for part in range(2):
+            total = term[2 * m + which, part].astype(F32) + term_in[which, part].astype(F32)
+            spread = matmul(total.astype(BF16), place).astype(BF16)
+            if step == 0:
+                placed_out[part] = spread
+            else:
+                placed_mine[part] = spread
+        if step == 0:
+            send_placed.start()
+    send_shift.wait()
+    send_placed.wait()
+    shift = shift_in[0:1, :]
+    shift = jnp.broadcast_to(jnp.concatenate([shift] * (width // 128), 1), (height, width))
+    line = lax.broadcasted_iota(jnp.int32, (height, width), 0) + own_slot * height
+    zero = jnp.zeros((height, width), F32)
+    send_carry = copy(carry_out, carry_in, c_send, c_recv, upper)
+    for part in range(2):
+        mine, theirs = placed_mine[part].astype(F32), placed_in[part].astype(F32)
+        carry_out[part] = (
+            jnp.where(line < row_start, mine, zero) + jnp.where(line < shift, theirs, zero)
+        ).astype(BF16)
+        object_out[part] = jnp.where(line >= row_start, mine, zero) + jnp.where(
+            line >= shift, theirs, zero
+        )
+
+    @pl.when(has_upper)
+    def _():
+        send_carry.start()
+
+    for index in range(CHAIN_PARTS):
+        @pl.when(t < root)
+        def _():
+            down_to_lower(index).wait_recv()
+
+            @pl.when(has_lower)
+            def _():
+                down_to_lower(index).start()
+
+            down_to_sibling(index).start()
+
+        @pl.when(t > root)
+        def _():
+            down_to_upper(index).wait_recv()
+
+            @pl.when(has_upper)
+            def _():
+                down_to_upper(index).start()
+
+            down_to_sibling(index).start()
+
+        rows = part_rows(index)
+        target = pl.ds(pl.multiple_of(r * half + index * chunk, chunk), chunk)
+        probe_out[0, 0, target, :] = down[rows, :points].astype(F32)
+        probe_out[0, 1, target, :] = down[rows, points:].astype(F32)
+
+    for index in range(CHAIN_PARTS):
+        down_to_sibling(index).wait()
+        rows = part_rows(index)
+        target = pl.ds(pl.multiple_of((1 - r) * half + index * chunk, chunk), chunk)
+        probe_out[0, 0, target, :] = down_in[rows, :points].astype(F32)
+        probe_out[0, 1, target, :] = down_in[rows, points:].astype(F32)
+
+    @pl.when(has_lower)
+    def _():
+        send_carry.wait_recv()
+        object_out[...] += carry_in[...].astype(F32)
+
+    @pl.when(has_upper)
+    def _():
+        send_carry.wait_send()
+
+    for index in range(CHAIN_PARTS):
+        @pl.when(t < root)
+        def _():
+            up_to_upper(index).wait_send()
+
+        @pl.when(t > root)
+        def _():
+            up_to_lower(index).wait_send()
+
+        @pl.when((t <= root) & has_lower)
+        def _():
+            down_to_lower(index).wait_send()
+
+        @pl.when((t >= root) & has_upper)
+        def _():
+            down_to_upper(index).wait_send()
+
+
+def fused_local(tiles, object_tiles, probe_modes, measured, row_offset, col_offset):
+    points = probe_modes.shape[-1]
+    height, width = object_tiles.shape[1:]
+    cosine, sine = (jnp.asarray(table) for table in cos_sin_tables(points))
+    double, half = 2 * points, points // 2
+    steps = points // POWER_ROWS
+    vmem, smem = pl.BlockSpec(memory_space=pltpu.VMEM), pl.BlockSpec(memory_space=pltpu.SMEM)
+    dma = pltpu.SemaphoreType.DMA
+    scratch = [
+        pltpu.VMEM((8, 2, height, width), BF16),
+        pltpu.VMEM((8, 128), jnp.int32),
+        pltpu.VMEM((8, 128), jnp.int32),
+        pltpu.VMEM((points, points), BF16),
+        pltpu.VMEM((points, points), BF16),
+        pltpu.VMEM((double, double), BF16),
+        pltpu.VMEM((double, double), BF16),
+        pltpu.VMEM((double, double), BF16),
+        pltpu.VMEM((double, double), BF16),
+        pltpu.VMEM((2, points, points), BF16),
+        pltpu.VMEM((2, points, points), BF16),
+        pltpu.VMEM((double, points), BF16),
+        pltpu.VMEM((points, double), BF16),
+        pltpu.VMEM((points, double), F32),
+        pltpu.VMEM((steps, POWER_ROWS, points), BF16),
+        pltpu.VMEM((steps, POWER_ROWS, points), BF16),
+        pltpu.VMEM((double, points), BF16),
+        pltpu.VMEM((4, 2, height, points), BF16),
+        pltpu.VMEM((2, 2, height, points), BF16),
+        pltpu.VMEM((points, double), BF16),
+        pltpu.VMEM((half, double), BF16),
+        pltpu.VMEM((half, double), BF16),
+        pltpu.VMEM((half, double), F32),
+        pltpu.VMEM((half, double), BF16),
+        pltpu.VMEM((half, double), BF16),
+        pltpu.VMEM((half, double), BF16),
+        pltpu.VMEM((half, double), BF16),
+        pltpu.VMEM((half, double), BF16),
+        pltpu.VMEM((2, height, width), BF16),
+        pltpu.VMEM((2, height, width), BF16),
+        pltpu.VMEM((2, height, width), BF16),
+        pltpu.VMEM((2, height, width), BF16),
+        pltpu.VMEM((2, height, width), BF16),
+        dma((7, 2)), dma((7, 2)), dma, dma, dma((steps,)), dma((steps,)), dma((2,)), dma((2,)),
+        dma, dma, dma((CHAIN_PARTS,)), dma((2, CHAIN_PARTS)), dma((2, CHAIN_PARTS)),
+        dma((CHAIN_PARTS,)), dma((CHAIN_PARTS,)), dma((CHAIN_PARTS,)), dma, dma, dma, dma,
+    ]
+    return pl.pallas_call(
+        functools.partial(fused_kernel, tiles),
+        out_shape=(
+            jax.ShapeDtypeStruct((2, height, width), F32),
+            jax.ShapeDtypeStruct((1, 2, points, points), F32),
+        ),
+        in_specs=[smem, smem, vmem, vmem, vmem, vmem, vmem],
+        out_specs=(vmem, vmem),
+        scratch_shapes=scratch,
+        compiler_params=pltpu.CompilerParams(
+            collective_id=0, has_side_effects=True, vmem_limit_bytes=56 * 1024 * 1024
+        ),
+    )(row_offset, col_offset, object_tiles, probe_modes, cosine, sine, measured)
+
+
 def solution(mesh):
     placed = (
         P(None, ("groups", "tile", "mode", "rep"), None),
@@ -131,8 +645,12 @@
         P(("groups", "tile", "rep")),
         P(("groups", "tile", "rep")),
     )
+    if mesh.shape["mode"] == 2 and mesh.shape["rep"] == 2:
+        body = functools.partial(fused_local, mesh.shape["tile"])
+    else:
+        body = local
     return jax.shard_map(
-        local,
+        body,
         mesh=mesh,
         in_specs=placed,
         out_specs=(

time: 273 us -> 82.5 us (0.30)
  waiting for transfers between devices: 168 us -> 0 us
  Pallas kernels: 0 us -> 75.3 us
  other arithmetic: 37.5 us -> 0 us
  matrix products: 25.3 us -> 0 us
  local copies, waits for them, and re-layouts: 20.8 us -> 5.05 us
  between operations: 15.2 us -> 1.93 us
  starting transfers between devices: 4.86 us -> 0 us
    psum x2 -> x0, waiting for transfers between devices: 86.1 us -> none  [the longest x1 58.3 us: local(): lax.psum(probe_term.astype(jnp.bfloat16), ('tile', 'rep'))]
    pallas_call x0 -> x1, Pallas kernels: none -> 75.3 us  [fused_local(): pl.pallas_call(functools.partial(fused_kernel, tiles), out_shape=(jax.Sha...]
    reduce_scatter x2 -> x0, waiting for transfers between devices: 49 us -> none  [the longest x1 25.1 us: local(): lax.psum_scatter(extended_term[:, :tile_rows].astype(jnp.bfloat16), ('mod...]
    dot_general x6 -> x0, matrix products: 25.3 us -> none  [the longest x2 11.5 us: row_pass(): jnp.dot(flattened, cos_table, preferred_element_type=jnp.float32)]
    all_gather x1 -> x0, waiting for transfers between devices: 22.5 us -> none  [local(): own_rows = lax.all_gather(object_tiles, ('mode', 'rep'), axis=1, tiled=True)]
    dynamic_update_slice x1 -> x0, local copies, waits for them, and re-layouts: 17 us -> none  [local(): lax.dynamic_update_slice(extended_term, obj_term, (zero_index, row_start,...]
    convert_element_type x6 -> x0, other arithmetic: 12.2 us -> none  [the longest x1 4.39 us: dft_tables(): sin_table = (jnp.sin(angles) * norm_factor).astype(jnp.bfloat16)]
    concatenate x1 -> x0, other arithmetic: 9.71 us -> none  [dft_tables(): jnp.concatenate([jnp.concatenate([cos_table, sin_table], 1), jnp.concaten...]
  transfers between devices with their start and end apart: 7 -> 0, of which waited for: 6 -> 0; matrix products, arithmetic and copies ran while one was open for 10% -> 0% of each run, Pallas kernels for 0% -> 0%
where the time goes in v1:
time: 82.5 us; the launch traced here: 82.3 us
  Pallas kernels  75.3 us (91%)
  local copies, waits for them, and re-layouts  5.05 us (6%)
  between operations  1.93 us (2%)
    pallas_call x1, Pallas kernels, fused_local(): pl.pallas_call(functools.partial(fused_kernel, tiles), out_shape=(jax.Sha...  75.3 us
    unnamed x2, local copies, waits for them, and re-layouts  5.05 us

profile of v1, /device:TPU:0, one launch (start us, length us, event | category | flops | bytes accessed | tf_op | source)
XLA Modules:
  0.0 82.3 jit_solution(5126877939534011671)
XLA Ops:
  1.9 75.3 %shard_map.86 = (f32[2,128,640]{2,1,0:T(8,128)}, f32[1,2,512,512]{3,2,1,0:T(8,128)}) custom-call(s32[1]{0:T(128)S(6)} %copy.11.row_ref, s32[1]{0:T(128)S(6)} %copy.12.col_ref, bf16[2,128,640]{2,1,0:T(8,128)(2,1)} %obj.1, bf16[1,2,512,512]{3,2,1,0:T(8,128)(2,1)} %probe.1, bf16[512,512]{1,0:T(8,128)(2,1)} %constant.4.clone.cos_ref, ...), custom_call_target="tpu_custom_call" | custom-call | tf_op jit(solution)/shard_map/pallas_call | solution.py:625
  77.2 2.0 %copy.13 = f32[2,128,640]{2,1,0:T(8,128)} copy(f32[2,128,640]{2,1,0:T(8,128)} %get-tuple-element.4) | data formatting | bytes 1310720
  79.2 3.1 %copy.14 = f32[1,2,512,512]{3,2,1,0:T(8,128)} copy(f32[1,2,512,512]{3,2,1,0:T(8,128)} %get-tuple-element.5) | data formatting | bytes 4194304

commit v2 on v1

--- a/solution.py
+++ b/solution.py
@@ -12,7 +12,9 @@
 PATCH = 512
 F32, BF16 = jnp.float32, jnp.bfloat16
 POWER_ROWS = 128
-CHAIN_PARTS = 4
+CHAIN_PARTS = 16
+CHAIN_LAG = 6
+GATHER_PARTS = 4
 
 def passed_along(value, axis, steps):
     count = lax.axis_size(axis)
@@ -148,12 +150,13 @@
 
 
 def fused_kernel(
-    tiles, row_ref, col_ref, obj, probe, cos_ref, sin_ref, measured, object_out, probe_out,
+    tiles, row_ref, col_ref, obj, probe_hbm, cos_hbm, sin_hbm, measured_hbm, object_out, probe_out,
+    probe, cos_ref, sin_ref, measured,
     ext, shift_out, shift_in, rotate, rotate_back, left_fwd, right_fwd, right_inv, left_inv,
     probe_rot, patch, wave, middle, spec, power, power_in, back_stack, term, term_in,
     probe_term, half_out, half_in, half_sum, up_left, up_right, up_out, down, down_in,
-    placed_out, placed_mine, placed_in, carry_out, carry_in,
-    g_send, g_recv, s_send, s_recv, pw_send, pw_recv, t_send, t_recv, h_send, h_recv,
+    placed_out, placed_mine, placed_in, carry_out, carry_in, own_sum,
+    g_send, g_recv, s_send, s_recv, pw_send, pw_recv, t_send, t_recv, h_send, h_recv, load,
     up_send, up_recv, dn_send, dn_recv, sib_send, sib_recv, pl_send, pl_recv, c_send, c_recv,
 ):
     t, m, r = lax.axis_index("tile"), lax.axis_index("mode"), lax.axis_index("rep")
@@ -162,6 +165,7 @@
     has_lower, has_upper = t > 0, t < tiles - 1
     height, width = obj.shape[1], obj.shape[2]
     points = probe.shape[-1]
+    piece = 2 * height // GATHER_PARTS
     row_start, col_start = row_ref[0], col_ref[0]
 
     def copy(src, dst, send, recv, device):
@@ -170,6 +174,19 @@
             device_id=device, device_id_type=pl.DeviceIdType.MESH,
         )
 
+    own_slot, other_slot = 2 * m + r, 2 * (1 - m) + r
+    loads = [
+        pltpu.make_async_copy(src, dst, load.at[index])
+        for index, (src, dst) in enumerate(
+            (
+                (probe_hbm, probe), (cos_hbm, cos_ref), (sin_hbm, sin_ref),
+                (measured_hbm, measured), (obj, ext.at[own_slot]),
+            )
+        )
+    ]
+    for one in loads:
+        one.start()
+
     barrier = pltpu.get_barrier_semaphore()
     for device in (sibling, partner):
         pl.semaphore_signal(barrier, inc=1, device_id=device, device_id_type=pl.DeviceIdType.MESH)
@@ -185,22 +202,24 @@
     peers = 2 + has_lower.astype(jnp.int32) + has_upper.astype(jnp.int32)
     pl.semaphore_wait(barrier, peers)
 
-    own_slot, other_slot = 2 * m + r, 2 * (1 - m) + r
+
+    def lines(part):
+        return part // (GATHER_PARTS // 2), pl.ds(part % (GATHER_PARTS // 2) * piece, piece)
 
     def gather(kind, part, src, slot, device):
-        return copy(src, ext.at[slot, part], g_send.at[kind, part], g_recv.at[kind, part], device)
+        return copy(src, ext.at[slot, *lines(part)], g_send.at[kind, part], g_recv.at[kind, part], device)
 
     def block(slot, part):
-        return ext.at[slot, part]
+        return ext.at[slot, *lines(part)]
 
     def to_sibling(part):
-        return gather(0, part, obj.at[part], own_slot, sibling)
+        return gather(0, part, obj.at[*lines(part)], own_slot, sibling)
 
     def to_partner(part):
-        return gather(1, part, obj.at[part], own_slot, partner)
+        return gather(1, part, obj.at[*lines(part)], own_slot, partner)
 
     def to_lower(part):
-        return gather(2, part, obj.at[part], 4 + own_slot, lower)
+        return gather(2, part, obj.at[*lines(part)], 4 + own_slot, lower)
 
     def relay_partner(part):
         return gather(3, part, block(other_slot, part), other_slot, sibling)
@@ -217,7 +236,7 @@
     def relay_cross(part):
         return gather(6, part, block(4 + other_slot, part), 4 + other_slot, sibling)
 
-    for part in range(2):
+    for part in range(GATHER_PARTS):
         to_partner(part).start()
 
         @pl.when(has_lower)
@@ -235,6 +254,8 @@
     rotate[...] = jnp.where((apart == 0) | (apart == -points), 1.0, 0.0).astype(BF16)
     apart = second - first - row_start
     rotate_back[...] = jnp.where((apart == 0) | (apart == -points), 1.0, 0.0).astype(BF16)
+    for one in loads[:3]:
+        one.wait()
     cosine, sine = cos_ref[...], sin_ref[...]
     minus = -sine
     right_fwd[:points, :points] = cosine
@@ -266,7 +287,8 @@
         for part in range(2):
             probe_rot[part, rows, :] = matmul(turn, probe[0, part]).astype(BF16)
 
-    ext[own_slot] = obj[...]
+    for one in loads[3:]:
+        one.wait()
 
     @pl.when(jnp.logical_not(has_upper))
     def _():
@@ -280,8 +302,8 @@
     def _():
         up_right[...] = jnp.zeros_like(up_right)
 
-    for part in range(2):
-        gather(1, part, obj.at[part], other_slot, partner).wait_recv()
+    for part in range(GATHER_PARTS):
+        gather(1, part, obj.at[*lines(part)], other_slot, partner).wait_recv()
         relay_partner(part).start()
 
         @pl.when((r == 1) & has_lower)
@@ -290,69 +312,79 @@
 
         @pl.when(has_upper)
         def _():
-            gather(2, part, obj.at[part], 4 + own_slot, lower).wait_recv()
+            gather(2, part, obj.at[*lines(part)], 4 + own_slot, lower).wait_recv()
             relay_upper(part).start()
 
             @pl.when(r == 0)
             def _():
                 cross_partner(part).start()
 
-    for part in range(2):
+    for part in range(GATHER_PARTS):
+        to_sibling(part).wait_recv()
+
         @pl.when(has_upper)
         def _():
-            gather(5, part, obj.at[part], 4 + other_slot, partner).wait_recv()
-            relay_cross(part).start()
-
-    for part in range(2):
-        to_sibling(part).wait()
-        to_partner(part).wait_send()
-        relay_partner(part).wait()
-
-        @pl.when(has_lower)
-        def _():
-            to_lower(part).wait_send()
-
-        @pl.when((r == 1) & has_lower)
-        def _():
-            cross_lower(part).wait_send()
-
-        @pl.when(has_upper)
-        def _():
-            relay_upper(part).wait()
-            relay_cross(part).wait()
-
-        @pl.when((r == 0) & has_upper)
-        def _():
-            cross_partner(part).wait_send()
+            relay_upper(part).wait_recv()
 
     pick = lax.broadcasted_iota(jnp.int32, (width, points), 0) - lax.broadcasted_iota(
         jnp.int32, (width, points), 1
     )
     pick = jnp.where(pick == col_start, 1.0, 0.0).astype(BF16)
 
-    @pl.loop(0, 4)
-    def _(step):
-        rows = rows_at(step * height, height)
-        low = rows_at(points + step * height, height)
-        line = lax.broadcasted_iota(jnp.int32, (height, width), 0) + step * height
-        parts = []
-        for part in range(2):
-            chosen = jnp.where(
-                line >= row_start, ext[step, part].astype(F32), ext[4 + step, part].astype(F32)
-            )
-            parts.append(matmul(chosen.astype(BF16), pick))
-            patch[part, rows, :] = parts[part].astype(BF16)
-        obj_re, obj_im = parts
-        prb_re, prb_im = (probe_rot[part, rows, :].astype(F32) for part in range(2))
-        wave[rows, :] = (prb_re * obj_re - prb_im * obj_im).astype(BF16)
-        wave[low, :] = (prb_re * obj_im + prb_im * obj_re).astype(BF16)
+    def exit_rows(side):
+        @pl.loop(0, 2)
+        def _(index):
+            step = 2 * side + index
+            rows = rows_at(step * height, height)
+            low = rows_at(points + step * height, height)
+            line = lax.broadcasted_iota(jnp.int32, (height, width), 0) + step * height
+            parts = []
+            for part in range(2):
+                chosen = jnp.where(
+                    line >= row_start, ext[step, part].astype(F32), ext[4 + step, part].astype(F32)
+                )
+                parts.append(matmul(chosen.astype(BF16), pick))
+                patch[part, rows, :] = parts[part].astype(BF16)
+            obj_re, obj_im = parts
+            prb_re, prb_im = (probe_rot[part, rows, :].astype(F32) for part in range(2))
+            wave[rows, :] = (prb_re * obj_re - prb_im * obj_im).astype(BF16)
+            wave[low, :] = (prb_re * obj_im + prb_im * obj_re).astype(BF16)
+
+    def column_part(rows, side):
+        near = rows_at(2 * side * height, 2 * height)
+        far = rows_at(points + 2 * side * height, 2 * height)
+        return matmul(left_fwd[rows, near], wave[near, :]) + matmul(left_fwd[rows, far], wave[far, :])
+
+    exit_rows(m)
 
     @pl.loop(0, 2)
     def _(step):
         rows = rows_at(step * 256, 256)
         low = rows_at(points + step * 256, 256)
-        middle[rows, :points] = matmul(left_fwd[rows, :], wave[...]).astype(BF16)
-        middle[rows, points:] = matmul(left_fwd[low, :], wave[...]).astype(BF16)
+        spec[rows, :points] = column_part(rows, m)
+        spec[rows, points:] = column_part(low, m)
+
+    for part in range(GATHER_PARTS):
+        @pl.when(has_upper)
+        def _():
+            gather(5, part, obj.at[*lines(part)], 4 + other_slot, partner).wait_recv()
+            relay_cross(part).start()
+
+    for part in range(GATHER_PARTS):
+        relay_partner(part).wait_recv()
+
+        @pl.when(has_upper)
+        def _():
+            relay_cross(part).wait_recv()
+
+    exit_rows(1 - m)
+
+    @pl.loop(0, 2)
+    def _(step):
+        rows = rows_at(step * 256, 256)
+        low = rows_at(points + step * 256, 256)
+        middle[rows, :points] = (spec[rows, :points] + column_part(rows, 1 - m)).astype(BF16)
+        middle[rows, points:] = (spec[rows, points:] + column_part(low, 1 - m)).astype(BF16)
 
     def send_power(step):
         return copy(
@@ -384,9 +416,32 @@
         back_stack[rows, :] = turned[:, :points]
         back_stack[low, :] = turned[:, points:]
 
-    def send_term(step):
+    for part in range(GATHER_PARTS):
+        to_sibling(part).wait_send()
+        to_partner(part).wait_send()
+        relay_partner(part).wait_send()
+
+        @pl.when(has_lower)
+        def _():
+            to_lower(part).wait_send()
+
+        @pl.when((r == 1) & has_lower)
+        def _():
+            cross_lower(part).wait_send()
+
+        @pl.when(has_upper)
+        def _():
+            relay_upper(part).wait_send()
+            relay_cross(part).wait_send()
+
+        @pl.when((r == 0) & has_upper)
+        def _():
+            cross_partner(part).wait_send()
+
+    def send_term(which, part):
         return copy(
-            term.at[2 * (1 - m) + step], term_in.at[step], t_send.at[step], t_recv.at[step], partner
+            term.at[2 * (1 - m) + which, part], term_in.at[which, part],
+            t_send.at[which, part], t_recv.at[which, part], partner,
         )
 
     @pl.loop(0, 4)
@@ -400,9 +455,11 @@
         term[slot, 0] = (prb_re * back_re + prb_im * back_im).astype(BF16)
         term[slot, 1] = (prb_re * back_im - prb_im * back_re).astype(BF16)
 
-        @pl.when(step < 2)
-        def _():
-            send_term(step).start()
+        @pl.when(step == 1)
+        def _():
+            for part in range(2):
+                send_term(1 - r, part).start()
+                send_term(r, part).start()
 
         obj_re, obj_im = (patch[part, rows, :].astype(F32) for part in range(2))
         probe_term[rows, :points] = (obj_re * back_re + obj_im * back_im).astype(BF16)
@@ -419,7 +476,7 @@
     root = tiles // 2
 
     def part_rows(index):
-        return pl.ds(index * chunk, chunk)
+        return pl.ds(pl.multiple_of(index * chunk, chunk), chunk)
 
     def up_to_upper(index):
         rows = part_rows(index)
@@ -441,7 +498,7 @@
         rows = part_rows(index)
         return copy(down.at[rows], down_in.at[rows], sib_send.at[index], sib_recv.at[index], sibling)
 
-    for index in range(CHAIN_PARTS):
+    def chain_up(index):
         rows = part_rows(index)
 
         @pl.when((t <= root) & has_lower)
@@ -476,95 +533,98 @@
             def _():
                 down_to_upper(index).start()
 
-            down_to_sibling(index).start()
+    def chain_down(index):
+        @pl.when(t < root)
+        def _():
+            down_to_lower(index).wait_recv()
+
+            @pl.when(has_lower)
+            def _():
+                down_to_lower(index).start()
+
+        @pl.when(t > root)
+        def _():
+            down_to_upper(index).wait_recv()
+
+            @pl.when(has_upper)
+            def _():
+                down_to_upper(index).start()
+
+        down_to_sibling(index).start()
+        target = pl.ds(pl.multiple_of(r * half + index * chunk, chunk), chunk)
+        rows = part_rows(index)
+        probe_out[0, 0, target, :] = down[rows, :points]
+        probe_out[0, 1, target, :] = down[rows, points:]
+
+    def chain(start, stop):
+        @pl.loop(start, stop)
+        def _(index):
+            chain_up(index)
+            chain_down(index - CHAIN_LAG)
 
     place = lax.broadcasted_iota(jnp.int32, (points, width), 1) - lax.broadcasted_iota(
         jnp.int32, (points, width), 0
     )
     place = jnp.where(place == col_start, 1.0, 0.0).astype(BF16)
-    send_placed = copy(placed_out, placed_in, pl_send, pl_recv, sibling)
-    for step in range(2):
-        send_term(step).wait()
-    for step in range(2):
-        which = 1 - r if step == 0 else r
-        for part in range(2):
+    line = lax.broadcasted_iota(jnp.int32, (height, width), 0) + own_slot * height
+
+    def send_placed(part):
+        return copy(
+            placed_out.at[part], placed_in.at[part], pl_send.at[part], pl_recv.at[part], sibling
+        )
+
+    def send_carry(part):
+        return copy(carry_out.at[part], carry_in.at[part], c_send.at[part], c_recv.at[part], upper)
+
+    def object_part(part):
+        for which, target in ((1 - r, placed_out), (r, placed_mine)):
+            send_term(which, part).wait()
             total = term[2 * m + which, part].astype(F32) + term_in[which, part].astype(F32)
-            spread = matmul(total.astype(BF16), place).astype(BF16)
-            if step == 0:
-                placed_out[part] = spread
-            else:
-                placed_mine[part] = spread
-        if step == 0:
-            send_placed.start()
-    send_shift.wait()
-    send_placed.wait()
-    shift = shift_in[0:1, :]
-    shift = jnp.broadcast_to(jnp.concatenate([shift] * (width // 128), 1), (height, width))
-    line = lax.broadcasted_iota(jnp.int32, (height, width), 0) + own_slot * height
-    zero = jnp.zeros((height, width), F32)
-    send_carry = copy(carry_out, carry_in, c_send, c_recv, upper)
-    for part in range(2):
+            target[part] = matmul(total.astype(BF16), place).astype(BF16)
+            if target is placed_out:
+                send_placed(part).start()
+        send_placed(part).wait()
+        shift = shift_in[0:1, :]
+        shift = jnp.broadcast_to(jnp.concatenate([shift] * (width // 128), 1), (height, width))
+        zero = jnp.zeros((height, width), F32)
         mine, theirs = placed_mine[part].astype(F32), placed_in[part].astype(F32)
         carry_out[part] = (
             jnp.where(line < row_start, mine, zero) + jnp.where(line < shift, theirs, zero)
         ).astype(BF16)
-        object_out[part] = jnp.where(line >= row_start, mine, zero) + jnp.where(
+
+        @pl.when(has_upper)
+        def _():
+            send_carry(part).start()
+
+        own_sum[part] = jnp.where(line >= row_start, mine, zero) + jnp.where(
             line >= shift, theirs, zero
         )
 
-    @pl.when(has_upper)
-    def _():
-        send_carry.start()
-
-    for index in range(CHAIN_PARTS):
+    @pl.loop(0, CHAIN_LAG)
+    def _(index):
+        chain_up(index)
+
+    chain(CHAIN_LAG, 8)
+    send_shift.wait()
+    object_part(0)
+    chain(8, 13)
+    object_part(1)
+    chain(13, CHAIN_PARTS)
+
+    @pl.loop(CHAIN_PARTS - CHAIN_LAG, CHAIN_PARTS)
+    def _(index):
+        chain_down(index)
+
+    @pl.loop(0, CHAIN_PARTS)
+    def _(index):
+        down_to_sibling(index).wait()
+
         @pl.when(t < root)
         def _():
-            down_to_lower(index).wait_recv()
-
-            @pl.when(has_lower)
-            def _():
-                down_to_lower(index).start()
-
-            down_to_sibling(index).start()
+            up_to_upper(index).wait_send()
 
         @pl.when(t > root)
         def _():
-            down_to_upper(index).wait_recv()
-
-            @pl.when(has_upper)
-            def _():
-                down_to_upper(index).start()
-
-            down_to_sibling(index).start()
-
-        rows = part_rows(index)
-        target = pl.ds(pl.multiple_of(r * half + index * chunk, chunk), chunk)
-        probe_out[0, 0, target, :] = down[rows, :points].astype(F32)
-        probe_out[0, 1, target, :] = down[rows, points:].astype(F32)
-
-    for index in range(CHAIN_PARTS):
-        down_to_sibling(index).wait()
-        rows = part_rows(index)
-        target = pl.ds(pl.multiple_of((1 - r) * half + index * chunk, chunk), chunk)
-        probe_out[0, 0, target, :] = down_in[rows, :points].astype(F32)
-        probe_out[0, 1, target, :] = down_in[rows, points:].astype(F32)
-
-    @pl.when(has_lower)
-    def _():
-        send_carry.wait_recv()
-        object_out[...] += carry_in[...].astype(F32)
-
-    @pl.when(has_upper)
-    def _():
-        send_carry.wait_send()
-
-    for index in range(CHAIN_PARTS):
-        @pl.when(t < root)
-        def _():
-            up_to_upper(index).wait_send()
-
-        @pl.when(t > root)
-        def _():
             up_to_lower(index).wait_send()
 
         @pl.when((t <= root) & has_lower)
@@ -574,6 +634,24 @@
         @pl.when((t >= root) & has_upper)
         def _():
             down_to_upper(index).wait_send()
+
+    target = rows_at((1 - r) * half, half)
+    probe_out[0, 0, target, :] = down_in[:, :points]
+    probe_out[0, 1, target, :] = down_in[:, points:]
+
+    for part in range(2):
+        @pl.when(has_lower)
+        def _():
+            send_carry(part).wait_recv()
+            object_out[part] = (own_sum[part] + carry_in[part].astype(F32)).astype(BF16)
+
+        @pl.when(jnp.logical_not(has_lower))
+        def _():
+            object_out[part] = own_sum[part].astype(BF16)
+
+        @pl.when(has_upper)
+        def _():
+            send_carry(part).wait_send()
 
 
 def fused_local(tiles, object_tiles, probe_modes, measured, row_offset, col_offset):
@@ -585,6 +663,10 @@
     vmem, smem = pl.BlockSpec(memory_space=pltpu.VMEM), pl.BlockSpec(memory_space=pltpu.SMEM)
     dma = pltpu.SemaphoreType.DMA
     scratch = [
+        pltpu.VMEM(probe_modes.shape, BF16),
+        pltpu.VMEM((points, points), BF16),
+        pltpu.VMEM((points, points), BF16),
+        pltpu.VMEM(measured.shape, F32),
         pltpu.VMEM((8, 2, height, width), BF16),
         pltpu.VMEM((8, 128), jnp.int32),
         pltpu.VMEM((8, 128), jnp.int32),
@@ -618,23 +700,25 @@
         pltpu.VMEM((2, height, width), BF16),
         pltpu.VMEM((2, height, width), BF16),
         pltpu.VMEM((2, height, width), BF16),
-        dma((7, 2)), dma((7, 2)), dma, dma, dma((steps,)), dma((steps,)), dma((2,)), dma((2,)),
-        dma, dma, dma((CHAIN_PARTS,)), dma((2, CHAIN_PARTS)), dma((2, CHAIN_PARTS)),
-        dma((CHAIN_PARTS,)), dma((CHAIN_PARTS,)), dma((CHAIN_PARTS,)), dma, dma, dma, dma,
+        pltpu.VMEM((2, height, width), F32),
+        dma((7, GATHER_PARTS)), dma((7, GATHER_PARTS)), dma, dma, dma((steps,)), dma((steps,)), dma((2, 2)), dma((2, 2)),
+        dma, dma, dma((5,)), dma((CHAIN_PARTS,)), dma((2, CHAIN_PARTS)), dma((2, CHAIN_PARTS)),
+        dma((CHAIN_PARTS,)), dma((CHAIN_PARTS,)), dma((CHAIN_PARTS,)), dma((2,)), dma((2,)), dma((2,)), dma((2,)),
     ]
-    return pl.pallas_call(
+    object_grad, probe_grad = pl.pallas_call(
         functools.partial(fused_kernel, tiles),
         out_shape=(
-            jax.ShapeDtypeStruct((2, height, width), F32),
-            jax.ShapeDtypeStruct((1, 2, points, points), F32),
+            jax.ShapeDtypeStruct((2, height, width), BF16),
+            jax.ShapeDtypeStruct((1, 2, points, points), BF16),
         ),
-        in_specs=[smem, smem, vmem, vmem, vmem, vmem, vmem],
+        in_specs=[smem, smem] + [pl.BlockSpec(memory_space=pl.ANY)] * 5,
         out_specs=(vmem, vmem),
         scratch_shapes=scratch,
         compiler_params=pltpu.CompilerParams(
             collective_id=0, has_side_effects=True, vmem_limit_bytes=56 * 1024 * 1024
         ),
     )(row_offset, col_offset, object_tiles, probe_modes, cosine, sine, measured)
+    return object_grad.astype(F32), probe_grad.astype(F32)
 
 
 def solution(mesh):

time: 82.5 us -> 129 us (1.56)
  Pallas kernels: 75.3 us -> 123 us
  local copies, waits for them, and re-layouts: 5.05 us -> 0.01 us
  other arithmetic: 0 us -> 3.76 us
    pallas_call x1, Pallas kernels: 75.3 us -> 123 us  [fused_local(): pl.pallas_call(functools.partial(fused_kernel, tiles), out_shape=(jax.Sha...]
    unnamed x2, local copies, waits for them, and re-layouts: 5.05 us -> 0.01 us
    convert_element_type x0 -> x2, other arithmetic: none -> 3.76 us  [fused_local(): return (object_grad.astype(F32), probe_grad.astype(F32))]
where the time goes in v2:
time: 129 us
  Pallas kernels  123 us (95%)
  other arithmetic  3.76 us (3%)
  between operations  1.94 us (2%)
    pallas_call x1, Pallas kernels, fused_local(): pl.pallas_call(functools.partial(fused_kernel, tiles), out_shape=(jax.Sha...  123 us
    convert_element_type x2, other arithmetic, fused_local(): return (object_grad.astype(F32), probe_grad.astype(F32))  3.76 us

profile of v2, /device:TPU:0, one launch (start us, length us, event | category | flops | bytes accessed | tf_op | source)
XLA Modules:
  0.0 129.0 jit_solution(6370040382025756048)
XLA Ops:
  1.9 123.3 %shard_map.86 = (bf16[2,128,640]{2,1,0:T(8,128)(2,1)}, bf16[1,2,512,512]{3,2,1,0:T(8,128)(2,1)}) custom-call(s32[1]{0:T(128)S(6)} %copy.9.row_ref, s32[1]{0:T(128)S(6)} %copy.10.col_ref, bf16[2,128,640]{2,1,0:T(8,128)(2,1)} %obj.1, bf16[1,2,512,512]{3,2,1,0:T(8,128)(2,1)} %probe_hbm.1, bf16[512,512]{1,0:T(8,128)(2,1)} %constant.4.clone.cos_hbm, ...), custom_call_target="tpu_custom_call" | custom-call | tf_op jit(solution)/shard_map/pallas_call | solution.py:708
  125.3 0.0 copy-start
  125.3 2.9 %convert_element_type.7 = f32[1,2,512,512]{3,2,1,0:T(8,128)} convert(bf16[1,2,512,512]{3,2,1,0:T(8,128)(2,1)} %get-tuple-element.5) | non-fusion elementwise | flops 524288 | bytes 3145728 | tf_op jit(solution)/shard_map/convert_element_type | solution.py:721
  128.2 0.0 copy-done
  128.2 0.9 convert_element_type.6
Async XLA Ops:
  125.3 2.9 %copy-start = (bf16[2,128,640]{2,1,0:T(8,128)(2,1)S(1)}, bf16[2,128,640]{2,1,0:T(8,128)(2,1)}, u32[]{:S(2)}) copy-start(bf16[2,128,640]{2,1,0:T(8,128)(2,1)} %get-tuple-element.4) | copy-start | bytes 983044

commit v3 on v2

--- a/solution.py
+++ b/solution.py
@@ -13,7 +13,7 @@
 F32, BF16 = jnp.float32, jnp.bfloat16
 POWER_ROWS = 128
 CHAIN_PARTS = 16
-CHAIN_LAG = 6
+CHAIN_LAG = 7
 GATHER_PARTS = 4
 
 def passed_along(value, axis, steps):
@@ -556,11 +556,20 @@
         probe_out[0, 0, target, :] = down[rows, :points]
         probe_out[0, 1, target, :] = down[rows, points:]
 
+    ends = (t == 0) | (t == tiles - 1)
+    lag = CHAIN_LAG * jnp.abs(t - root)
+    chain_steps = CHAIN_PARTS + CHAIN_LAG * max(root, tiles - 1 - root)
+
     def chain(start, stop):
         @pl.loop(start, stop)
         def _(index):
-            chain_up(index)
-            chain_down(index - CHAIN_LAG)
+            @pl.when((index < CHAIN_PARTS) & jnp.logical_not(ends & (t != root)))
+            def _():
+                chain_up(index)
+
+            @pl.when((index >= lag) & (index < lag + CHAIN_PARTS))
+            def _():
+                chain_down(index - lag)
 
     place = lax.broadcasted_iota(jnp.int32, (points, width), 1) - lax.broadcasted_iota(
         jnp.int32, (points, width), 0
@@ -600,20 +609,18 @@
             line >= shift, theirs, zero
         )
 
-    @pl.loop(0, CHAIN_LAG)
-    def _(index):
-        chain_up(index)
-
-    chain(CHAIN_LAG, 8)
+    @pl.when(ends & (t != root))
+    def _():
+        @pl.loop(0, CHAIN_PARTS)
+        def _(index):
+            chain_up(index)
+
+    chain(0, 6)
     send_shift.wait()
     object_part(0)
-    chain(8, 13)
+    chain(6, 13)
     object_part(1)
-    chain(13, CHAIN_PARTS)
-
-    @pl.loop(CHAIN_PARTS - CHAIN_LAG, CHAIN_PARTS)
-    def _(index):
-        chain_down(index)
+    chain(13, chain_steps)
 
     @pl.loop(0, CHAIN_PARTS)
     def _(index):

time: 129 us -> 79.1 us (0.61)
  Pallas kernels: 123 us -> 73.2 us
    pallas_call x1, Pallas kernels: 123 us -> 73.2 us  [fused_local(): pl.pallas_call(functools.partial(fused_kernel, tiles), out_shape=(jax.Sha...]
where the time goes in v3:
time: 79.1 us; the launch traced here: 78.9 us
  Pallas kernels  73.2 us (93%)
  other arithmetic  3.76 us (5%)
  between operations  1.94 us (2%)
    pallas_call x1, Pallas kernels, fused_local(): pl.pallas_call(functools.partial(fused_kernel, tiles), out_shape=(jax.Sha...  73.2 us
    convert_element_type x2, other arithmetic, fused_local(): return (object_grad.astype(F32), probe_grad.astype(F32))  3.76 us

profile of v3, /device:TPU:0, one launch (start us, length us, event | category | flops | bytes accessed | tf_op | source)
XLA Modules:
  0.0 78.9 jit_solution(14587225127226762058)
XLA Ops:
  1.9 73.2 %shard_map.86 = (bf16[2,128,640]{2,1,0:T(8,128)(2,1)}, bf16[1,2,512,512]{3,2,1,0:T(8,128)(2,1)}) custom-call(s32[1]{0:T(128)S(6)} %copy.9.row_ref, s32[1]{0:T(128)S(6)} %copy.10.col_ref, bf16[2,128,640]{2,1,0:T(8,128)(2,1)} %obj.1, bf16[1,2,512,512]{3,2,1,0:T(8,128)(2,1)} %probe_hbm.1, bf16[512,512]{1,0:T(8,128)(2,1)} %constant.4.clone.cos_hbm, ...), custom_call_target="tpu_custom_call" | custom-call | tf_op jit(solution)/shard_map/pallas_call | solution.py:715
  75.1 0.0 copy-start
  75.1 2.9 %convert_element_type.7 = f32[1,2,512,512]{3,2,1,0:T(8,128)} convert(bf16[1,2,512,512]{3,2,1,0:T(8,128)(2,1)} %get-tuple-element.5) | non-fusion elementwise | flops 524288 | bytes 3145728 | tf_op jit(solution)/shard_map/convert_element_type | solution.py:728
  78.0 0.0 copy-done
  78.0 0.9 %convert_element_type.6 = f32[2,128,640]{2,1,0:T(8,128)} convert(bf16[2,128,640]{2,1,0:T(8,128)(2,1)S(1)} %copy-done) | non-fusion elementwise | flops 163840 | bytes 983040 | tf_op jit(solution)/shard_map/convert_element_type | solution.py:728
Async XLA Ops:
  75.1 2.9 %copy-start = (bf16[2,128,640]{2,1,0:T(8,128)(2,1)S(1)}, bf16[2,128,640]{2,1,0:T(8,128)(2,1)}, u32[]{:S(2)}) copy-start(bf16[2,128,640]{2,1,0:T(8,128)(2,1)} %get-tuple-element.4) | copy-start | bytes 983044

commit v4 on v3

--- a/solution.py
+++ b/solution.py
@@ -12,8 +12,9 @@
 PATCH = 512
 F32, BF16 = jnp.float32, jnp.bfloat16
 POWER_ROWS = 128
-CHAIN_PARTS = 16
-CHAIN_LAG = 7
+CHAIN_PARTS = 8
+CHAIN_LAG = 5
+IN_FLIGHT = 3
 GATHER_PARTS = 4
 
 def passed_along(value, axis, steps):
@@ -399,13 +400,21 @@
         wide = matmul(middle[rows, :], right_fwd[...])
         spec[rows, :] = wide
         power[step] = (wide[:, :points] ** 2 + wide[:, points:] ** 2).astype(BF16)
-        send_power(step).start()
+
+        @pl.when(step < IN_FLIGHT)
+        def _():
+            send_power(step).start()
 
     @pl.loop(0, steps)
     def _(step):
         rows = rows_at(step * POWER_ROWS, POWER_ROWS)
         low = rows_at(points + step * POWER_ROWS, POWER_ROWS)
         send_power(step).wait()
+
+        @pl.when(step + IN_FLIGHT < steps)
+        def _():
+            send_power(step + IN_FLIGHT).start()
+
         spec_re, spec_im = spec[rows, :points], spec[rows, points:]
         intensity = spec_re**2 + spec_im**2 + power_in[step].astype(F32)
         factor = 1.0 - measured[0, rows, :] / jnp.sqrt(jnp.maximum(intensity, 1.0))
@@ -457,9 +466,8 @@
 
         @pl.when(step == 1)
         def _():
-            for part in range(2):
-                send_term(1 - r, part).start()
-                send_term(r, part).start()
+            for which in (1 - r, r):
+                send_term(which, 0).start()
 
         obj_re, obj_im = (patch[part, rows, :].astype(F32) for part in range(2))
         probe_term[rows, :points] = (obj_re * back_re + obj_im * back_im).astype(BF16)
@@ -512,11 +520,21 @@
         @pl.when(t < root)
         def _():
             up_out[rows] = (half_sum[rows] + up_left[rows].astype(F32)).astype(BF16)
+
+            @pl.when(index >= IN_FLIGHT)
+            def _():
+                up_to_upper(index - IN_FLIGHT).wait_send()
+
             up_to_upper(index).start()
 
         @pl.when(t > root)
         def _():
             up_out[rows] = (half_sum[rows] + up_right[rows].astype(F32)).astype(BF16)
+
+            @pl.when(index >= IN_FLIGHT)
+            def _():
+                up_to_lower(index - IN_FLIGHT).wait_send()
+
             up_to_lower(index).start()
 
         @pl.when(t == root)
@@ -556,14 +574,13 @@
         probe_out[0, 0, target, :] = down[rows, :points]
         probe_out[0, 1, target, :] = down[rows, points:]
 
-    ends = (t == 0) | (t == tiles - 1)
     lag = CHAIN_LAG * jnp.abs(t - root)
     chain_steps = CHAIN_PARTS + CHAIN_LAG * max(root, tiles - 1 - root)
 
     def chain(start, stop):
         @pl.loop(start, stop)
         def _(index):
-            @pl.when((index < CHAIN_PARTS) & jnp.logical_not(ends & (t != root)))
+            @pl.when(index < CHAIN_PARTS)
             def _():
                 chain_up(index)
 
@@ -609,28 +626,25 @@
             line >= shift, theirs, zero
         )
 
-    @pl.when(ends & (t != root))
-    def _():
-        @pl.loop(0, CHAIN_PARTS)
-        def _(index):
-            chain_up(index)
-
-    chain(0, 6)
+    chain(0, 2)
+    for which in (1 - r, r):
+        send_term(which, 1).start()
+    chain(2, CHAIN_PARTS)
     send_shift.wait()
     object_part(0)
-    chain(6, 13)
+    chain(CHAIN_PARTS, CHAIN_PARTS + 1)
     object_part(1)
-    chain(13, chain_steps)
+    chain(CHAIN_PARTS + 1, chain_steps)
 
     @pl.loop(0, CHAIN_PARTS)
     def _(index):
         down_to_sibling(index).wait()
 
-        @pl.when(t < root)
+        @pl.when((t < root) & (index >= CHAIN_PARTS - IN_FLIGHT))
         def _():
             up_to_upper(index).wait_send()
 
-        @pl.when(t > root)
+        @pl.when((t > root) & (index >= CHAIN_PARTS - IN_FLIGHT))
         def _():
             up_to_lower(index).wait_send()
 

time: 79.1 us -> 73 us (0.923)
  Pallas kernels: 73.2 us -> 67.2 us
    pallas_call x1, Pallas kernels: 73.2 us -> 67.2 us  [fused_local(): pl.pallas_call(functools.partial(fused_kernel, tiles), out_shape=(jax.Sha...]
where the time goes in v4:
time: 73 us; the launch traced here: 72.9 us
  Pallas kernels  67.2 us (92%)
  other arithmetic  3.76 us (5%)
  between operations  1.94 us (3%)
    pallas_call x1, Pallas kernels, fused_local(): pl.pallas_call(functools.partial(fused_kernel, tiles), out_shape=(jax.Sha...  67.2 us
    convert_element_type x2, other arithmetic, fused_local(): return (object_grad.astype(F32), probe_grad.astype(F32))  3.76 us

profile of v4, /device:TPU:0, one launch (start us, length us, event | category | flops | bytes accessed | tf_op | source)
XLA Modules:
  0.0 72.9 jit_solution(2173277992178924734)
XLA Ops:
  1.9 67.2 %shard_map.86 = (bf16[2,128,640]{2,1,0:T(8,128)(2,1)}, bf16[1,2,512,512]{3,2,1,0:T(8,128)(2,1)}) custom-call(s32[1]{0:T(128)S(6)} %copy.9.row_ref, s32[1]{0:T(128)S(6)} %copy.10.col_ref, bf16[2,128,640]{2,1,0:T(8,128)(2,1)} %obj.1, bf16[1,2,512,512]{3,2,1,0:T(8,128)(2,1)} %probe_hbm.1, bf16[512,512]{1,0:T(8,128)(2,1)} %constant.4.clone.cos_hbm, ...), custom_call_target="tpu_custom_call" | custom-call | tf_op jit(solution)/shard_map/pallas_call | solution.py:729
  69.1 0.0 copy-start
  69.1 2.9 %convert_element_type.7 = f32[1,2,512,512]{3,2,1,0:T(8,128)} convert(bf16[1,2,512,512]{3,2,1,0:T(8,128)(2,1)} %get-tuple-element.5) | non-fusion elementwise | flops 524288 | bytes 3145728 | tf_op jit(solution)/shard_map/convert_element_type | solution.py:742
  72.0 0.0 copy-done
  72.0 0.9 %convert_element_type.6 = f32[2,128,640]{2,1,0:T(8,128)} convert(bf16[2,128,640]{2,1,0:T(8,128)(2,1)S(1)} %copy-done) | non-fusion elementwise | flops 163840 | bytes 983040 | tf_op jit(solution)/shard_map/convert_element_type | solution.py:742
Async XLA Ops:
  69.1 2.9 %copy-start = (bf16[2,128,640]{2,1,0:T(8,128)(2,1)S(1)}, bf16[2,128,640]{2,1,0:T(8,128)(2,1)}, u32[]{:S(2)}) copy-start(bf16[2,128,640]{2,1,0:T(8,128)(2,1)} %get-tuple-element.4) | copy-start | bytes 983044
